TPU v7x, 32 devices: a whole 2x2x4 slice. The times are simulated.
32 devices in a mesh: energy: 8 (over z, y), transpor: 4 (over x, core).
Axes of the slice: x: 2, y: 2, z: 4, core: 2. Of those that a mesh axis runs over, the one named last changes fastest.
Arguments:
- ham_diag: float32 [8, 2, 192, 192], P('transpor'), may hold values from -1 to 1, as said below
- ham_hop: float32 [8, 2, 192, 192], P('transpor'), may hold values from -1.3 to 1.3, as said below
- inject: float32 [8, 2, 192, 192], P('transpor'), may hold values from -4 to 4
- chemical: float32 [192], replicated, may hold values from -1 to 1
- energy_slot: int32 [8], P('energy'), may hold values from 0 to 7, each once
- onsite_shift: float32 [8, 8, 192], P('energy', 'transpor'), may hold values from -3 to 3
- onsite_loss: float32 [8, 8, 192], P('energy', 'transpor'), may hold values from 0.05 to 0.4
Outputs:
- polar: float32 [8, 8, 2, 192, 192], P('energy', 'transpor')
Inputs may be any that keep to these rules, and one draw needn't show every extreme that they name: `energy_slot`: every grid index 0 to 7 appears once. `ham_diag`: each block is Hermitian: real part symmetric, imaginary part antisymmetric. `ham_hop`: the diagonal of each block has real parts of 0.7 to 1.3 and imaginary parts 0.
All inputs are finite; a program needn't handle non-finite values.
Results may differ from a plain program's by a relative error of at most 0.0003.
Values sent between devices are 32-bit elements; how exact they have to be, the bound alone decides.
A program may use at most 128 MiB of HBM per device.

v0:
```python
import functools

import jax
import jax.numpy as jnp
from jax import lax
from jax.experimental import pallas as pl
from jax.experimental.pallas import tpu as pltpu
from jax.sharding import PartitionSpec as P

ENERGY_LOW = -1.5
ENERGY_SPAN = 3.0
THERMAL = 0.1
LOSS_FLOOR = 0.05
LANES = 128
MARGIN = 0.02


def one_term(left_op, right_op):
    return jnp.dot(left_op, right_op, preferred_element_type=jnp.float32)


def one_term_rows(left_op, right_op):
    dims = (((1,), (1,)), ((), ()))
    return lax.dot_general(left_op, right_op, dims, preferred_element_type=jnp.float32)


def split(value, count=2):
    parts = []
    for part in range(count):
        parts.append(value.astype(jnp.bfloat16))
        if part < count - 1:
            value = value - parts[-1].astype(jnp.float32)
    return parts


def multiply(left_op, right_op, dot=one_term):
    count = len(left_op)
    total = None
    for place in range(count - 1, -1, -1):
        for first in range(place + 1):
            term = dot(left_op[first], right_op[place - first])
            total = term if total is None else total + term
    return total


def ready(value, count=2):
    return tuple(split(part, count) for part in (value[0], value[1], value[0] + value[1]))


def cmul_ready(left_op, right_op):
    first = multiply(left_op[0], right_op[0])
    second = multiply(left_op[1], right_op[1])
    third = multiply(left_op[2], right_op[2])
    return first - second, third - first - second


def ready_turned(value):
    return tuple(split(part) for part in (value[0], value[1], value[0] - value[1]))


def cmul_turned(left_op, right_op):
    first = multiply(left_op[0], right_op[0], one_term_rows)
    second = multiply(left_op[1], right_op[1], one_term_rows)
    third = multiply(left_op[2], right_op[2], one_term_rows)
    return first + second, third - first + second


def adjoint(value):
    return jnp.transpose(value[0]), -jnp.transpose(value[1])


def on_diagonal_of(order):
    row = lax.broadcasted_iota(jnp.int32, (order, order), 0)
    column = lax.broadcasted_iota(jnp.int32, (order, order), 1)
    return row == column


def invert(matrix, x_ref):
    start = adjoint(matrix)
    matrix_ready = ready(matrix)
    gram = cmul_ready(matrix_ready, ready(start))
    high = jnp.max(jnp.sum(jnp.abs(gram[0]) + jnp.abs(gram[1]), axis=0, keepdims=True))
    inner = 1.0 / high

    def raised(low, scale):
        reach = scale * low
        return jnp.minimum(reach * (2.0 - reach), scale * (2.0 - scale))

    def scale_for(low):
        return 2.0 / (1.0 + jnp.maximum(low, MARGIN))

    def step(x, x_ready, product, scale, outer):
        change = cmul_ready(x_ready, ready(product))
        x_ref[0] = outer * (2.0 * x[0] - scale * change[0])
        x_ref[1] = outer * (2.0 * x[1] - scale * change[1])

    low = jnp.float32(0.98 * LOSS_FLOOR * LOSS_FLOOR) * inner
    scale = scale_for(low)
    step(start, ready(start), gram, scale * inner, scale * inner)
    low = raised(low, scale)

    def refine(low):
        x = (x_ref[0], x_ref[1])
        x_ready = ready(x)
        product = cmul_ready(matrix_ready, x_ready)
        scale = scale_for(low)
        step(x, x_ready, product, scale, scale)
        return raised(low, scale)

    low = lax.while_loop(lambda low: low < 0.998, refine, low)
    scale = 2.0 / (1.0 + low)
    x = (x_ref[0], x_ref[1])
    product = cmul_ready(ready(matrix, 3), ready(x, 3))
    aim = jnp.where(on_diagonal_of(matrix[0].shape[0]), 2.0 * scale - 1.0, 0.0)
    left_over = (aim - scale * scale * product[0], -(scale * scale) * product[1])
    change = cmul_ready(ready(x), ready(left_over))
    return x[0] + change[0], x[1] + change[1]


def take(ref, first):
    return ref[first], ref[first + 1]


def put(ref, first, value):
    ref[first] = value[0]
    ref[first + 1] = value[1]


def minus(left_op, right_op):
    return left_op[0] - right_op[0], left_op[1] - right_op[1]


def negated(value):
    return -value[0], -value[1]


def pick(left, first, second):
    return jnp.where(left, first[0], second[0]), jnp.where(left, first[1], second[1])


def couplings(left, hop, prev):
    behind = negated(adjoint((prev[0], prev[1])))
    within = negated(adjoint((hop[0, 0], hop[0, 1])))
    inner = negated((hop[0, 0], hop[0, 1]))
    onward = negated((hop[1, 0], hop[1, 1]))
    return (
        lambda: pick(left, behind, onward),
        lambda: pick(left, inner, within),
        lambda: pick(left, within, inner),
        lambda: pick(left, onward, behind),
    )


def eliminate_kernel(starts, partitions, carry, diag, hop, prev, inject, shift, loss, energy,
                     first_out, second_out, reduced_out, x_ref):
    my_index = lax.axis_index("transpor")
    left = my_index < partitions // 2
    is_last = jnp.where(my_index == partitions - 1, 1.0, 0.0)
    where_diag = on_diagonal_of(diag.shape[2])
    contact_op = (hop[1, 0], hop[1, 1])
    contact = cmul_turned(ready(contact_op), ready_turned(contact_op))
    blocks = []
    for block in range(2):
        level = energy[...] - shift[block : block + 1]
        block_re = jnp.where(where_diag, level, 0.0) - diag[block, 0]
        block_im = jnp.where(where_diag, loss[block : block + 1], 0.0) - diag[block, 1]
        if block == 1:
            block_re = block_re - is_last * contact[1]
            block_im = block_im + is_last * contact[0]
        blocks.append((block_re, block_im))
    low_a, up_a, low_b, up_b = couplings(left, hop, prev)
    sources = [(inject[block, 0], inject[block, 1]) for block in range(2)]

    pivot = pick(left, blocks[0], blocks[1])
    source = pick(left, sources[0], sources[1])
    if not starts:
        back = ready(low_a())
        pivot = minus(pivot, cmul_ready(back, ready(take(carry, 0))))
        source = minus(source, cmul_ready(back, ready(take(carry, 2))))
    put(reduced_out, 0, pick(left, blocks[1], blocks[0]))
    inverse = ready(invert(pivot, x_ref))
    on = cmul_ready(inverse, ready(up_a()))
    put(first_out, 0, on)
    held = cmul_ready(inverse, ready(source))
    put(first_out, 2, held)
    back = ready(low_b())
    pivot = minus(take(reduced_out, 0), cmul_ready(back, ready(on)))
    source = minus(pick(left, sources[1], sources[0]), cmul_ready(back, ready(held)))
    put(reduced_out, 0, pivot)
    put(reduced_out, 2, source)
    inverse = ready(invert(pivot, x_ref))
    put(second_out, 0, cmul_ready(inverse, ready(up_b())))
    put(second_out, 2, cmul_ready(inverse, ready(source)))


def join_kernel(partitions, carry, reduced, first, hop, prev, value_out, first_value_out, x_ref):
    left = lax.axis_index("transpor") < partitions // 2
    on = ready(couplings(left, hop, prev)[3]())
    pivot = minus(take(reduced, 0), cmul_ready(on, ready(take(carry, 0))))
    source = minus(take(reduced, 2), cmul_ready(on, ready(take(carry, 2))))
    inverse = ready(invert(pivot, x_ref))
    value = cmul_ready(inverse, ready(source))
    put(value_out, 0, value)
    change = cmul_ready(ready(take(first, 0)), ready(value))
    put(first_value_out, 0, minus(take(first, 2), change))


def back_kernel(value, second, first, second_out, first_out):
    change = cmul_ready(ready(take(second, 0)), ready(take(value, 0)))
    result = minus(take(second, 2), change)
    put(second_out, 0, result)
    change = cmul_ready(ready(take(first, 0)), ready(result))
    put(first_out, 0, minus(take(first, 2), change))


def place(half, offset):
    row = lax.broadcasted_iota(jnp.int32, (half, half), 0)
    column = lax.broadcasted_iota(jnp.int32, (half, half), 1)
    return row, column


def pack(block_re, block_im):
    half = block_re.shape[0] // 2
    row, column = place(half, 0)
    top_re, top_im = block_re[:half, :half], block_im[:half, :half]
    low_re, low_im = block_re[half:, half:], block_im[half:, half:]
    both_re = jnp.where(column >= row, top_re, low_re)
    both_im = jnp.where(column > row, top_im, jnp.where(column == row, low_re, low_im))
    return (
        jnp.concatenate([both_re, block_re[:half, half:]], axis=1),
        jnp.concatenate([both_im, block_im[:half, half:]], axis=1),
    )


def unpack(packed_re, packed_im):
    half = packed_re.shape[0]
    row, column = place(half, 0)
    both_re, side_re = packed_re[:, :half], packed_re[:, half:]
    both_im, side_im = packed_im[:, :half], packed_im[:, half:]
    turned_re, turned_im = jnp.transpose(both_re), -jnp.transpose(both_im)
    top_re = jnp.where(column >= row, both_re, turned_re)
    low_re = jnp.where(column < row, both_re, jnp.where(column == row, both_im, turned_re))
    top_im = jnp.where(column > row, both_im, jnp.where(column == row, 0.0, turned_im))
    low_im = jnp.where(column < row, both_im, jnp.where(column == row, 0.0, turned_im))
    whole_re = jnp.concatenate(
        [
            jnp.concatenate([top_re, side_re], axis=1),
            jnp.concatenate([jnp.transpose(side_re), low_re], axis=1),
        ],
        axis=0,
    )
    whole_im = jnp.concatenate(
        [
            jnp.concatenate([top_im, side_im], axis=1),
            jnp.concatenate([-jnp.transpose(side_im), low_im], axis=1),
        ],
        axis=0,
    )
    return whole_re, whole_im


def fold(first, second):
    half = first.shape[0]
    return jnp.concatenate(
        [
            first[:, :LANES],
            second[:, :LANES],
            jnp.concatenate([first[:, LANES:], second[:, LANES:]], axis=1),
        ],
        axis=0,
    )


def unfold(rows_of, half):
    tail = rows_of[2 * half :]
    side = tail.shape[1] // 2
    return (
        jnp.concatenate([rows_of[:half], tail[:, :side]], axis=1),
        jnp.concatenate([rows_of[half : 2 * half], tail[:, side:]], axis=1),
    )


def exchange_kernel(count, half_way, value_a, value_b, weight, slot, polar_out,
                    packed, arrived, ordered, sums, returned, merged,
                    out_sem, in_sem, back_sem, home_sem):
    me = lax.axis_index("energy")
    left = lax.axis_index("transpor") < half_way
    order = value_a.shape[1]
    half = order // 2
    rows = sums.shape[2]
    barrier = pltpu.get_barrier_semaphore()
    for step in range(1, count):
        pl.semaphore_signal(
            barrier,
            inc=1,
            device_id={"energy": lax.rem(me + step, count)},
            device_id_type=pl.DeviceIdType.MESH,
        )
    kinds = [[], []]
    for first, second in ((value_a, value_b), (value_b, value_a)):
        state_re = jnp.where(left, first[0], second[0])
        state_im = jnp.where(left, first[1], second[1])
        turned = ready_turned((state_re, state_im))
        for kind in range(2):
            held = weight[kind : kind + 1, :]
            weighted = ready((state_re * held, state_im * held))
            kinds[kind].append(pack(*cmul_turned(weighted, turned)))
    for kind in range(2):
        for part in range(2):
            flat = fold(kinds[kind][0][part], kinds[kind][1][part])
            for piece in range(count):
                packed[piece, 2 * kind + part, :rows] = flat[piece * rows : (piece + 1) * rows]
    for piece in range(count):
        for part in range(4):
            packed[piece, part, rows:] = slot[...]
    pl.semaphore_wait(barrier, count - 1)

    def there(step):
        other = lax.rem(me + step, count)
        return pltpu.make_async_remote_copy(
            src_ref=packed.at[other],
            dst_ref=arrived.at[me],
            send_sem=out_sem.at[step],
            recv_sem=in_sem.at[step],
            device_id={"energy": other},
            device_id_type=pl.DeviceIdType.MESH,
        )

    for step in range(1, count):
        there(step).start()
    arrived[me] = packed[me]
    for step in range(1, count):
        there(step).wait_recv()

    own = me * rows + lax.broadcasted_iota(jnp.int32, (rows, LANES), 0)
    lane = lax.broadcasted_iota(jnp.int32, (rows, LANES), 1)
    within = jnp.where(own >= half, own - half, own)
    on_diagonal = (own < order) & (lane == within)
    for position in range(count):
        total = [jnp.zeros((rows, LANES), jnp.float32)] * 4
        for source in range(count):
            here = arrived[source, 0, rows:] == position
            total = [
                jnp.where(here, arrived[source, part, :rows], total[part]) for part in range(4)
            ]
        ordered[position, 0] = total[0]
        ordered[position, 1] = total[1]
        ordered[position, 2] = total[2]
        ordered[position, 3] = jnp.where(on_diagonal, 0.0, total[3])
        ordered[position, 4] = jnp.where(on_diagonal, total[3], total[2])
    for lag in range(count):
        sum_re = jnp.zeros((rows, LANES), jnp.float32)
        sum_im = jnp.zeros((rows, LANES), jnp.float32)
        for position in range(lag, count):
            before = position - lag
            lesser_re, lesser_im = ordered[position, 0], ordered[position, 1]
            greater_im = ordered[before, 3]
            sum_re = sum_re + (lesser_re * ordered[before, 2] + lesser_im * greater_im)
            sum_im = sum_im + (lesser_im * ordered[before, 4] - lesser_re * greater_im)
        sums[lag, 0] = sum_re / count
        sums[lag, 1] = sum_im / count

    def back(step):
        other = lax.rem(me + step, count)
        return pltpu.make_async_remote_copy(
            src_ref=sums.at[other],
            dst_ref=returned.at[me],
            send_sem=back_sem.at[step],
            recv_sem=home_sem.at[step],
            device_id={"energy": other},
            device_id_type=pl.DeviceIdType.MESH,
        )

    for step in range(1, count):
        back(step).start()
    returned[me] = sums[me]
    for step in range(1, count):
        back(step).wait_recv()
    for piece in range(count):
        for part in range(2):
            merged[part, piece * rows : (piece + 1) * rows] = returned[piece, part]
    parts = [unfold(merged[part], half) for part in range(2)]
    for block in range(2):
        whole_re, whole_im = unpack(parts[0][block], parts[1][block])
        polar_out[0, block, 0] = whole_re
        polar_out[0, block, 1] = whole_im
    for step in range(1, count):
        there(step).wait_send()
        back(step).wait_send()


def exchange(value_a, value_b, weight, slot, count, half_way):
    order = value_a.shape[1]
    rows = order * order // LANES // count
    dma = pltpu.SemaphoreType.DMA((count,))
    return pl.pallas_call(
        functools.partial(exchange_kernel, count, half_way),
        out_shape=jax.ShapeDtypeStruct((1, 2, 2, order, order), jnp.float32),
        scratch_shapes=[
            pltpu.VMEM((count, 4, rows + 1, LANES), jnp.float32),
            pltpu.VMEM((count, 4, rows + 1, LANES), jnp.float32),
            pltpu.VMEM((count, 5, rows, LANES), jnp.float32),
            pltpu.VMEM((count, 2, rows, LANES), jnp.float32),
            pltpu.VMEM((count, 2, rows, LANES), jnp.float32),
            pltpu.VMEM((2, rows * count, LANES), jnp.float32),
            dma,
            dma,
            dma,
            dma,
        ],
        compiler_params=pltpu.CompilerParams(
            collective_id=0, has_side_effects=True, vmem_limit_bytes=48 * 1024 * 1024
        ),
    )(value_a, value_b, weight, slot)


def call(body, counts, order, scratch=True):
    shapes = [jax.ShapeDtypeStruct((count, order, order), jnp.float32) for count in counts]
    return pl.pallas_call(
        body,
        out_shape=shapes,
        scratch_shapes=[pltpu.VMEM((2, order, order), jnp.float32)] if scratch else [],
        compiler_params=pltpu.CompilerParams(vmem_limit_bytes=48 * 1024 * 1024),
    )


def passed_along(x, axis, by):
    length = lax.axis_size(axis)
    pairs = [(i, i + by) for i in range(length) if 0 <= i + by < length]
    return lax.ppermute(x, axis, pairs)


def per_device(ham_diag, ham_hop, inject, chemical, energy_slot, onsite_shift, onsite_loss):
    orbitals = ham_diag.shape[2]
    energies = energy_slot.shape[0]
    partitions = lax.axis_size("transpor")
    half = partitions // 2
    my_index = lax.axis_index("transpor")
    grid_total = energies * lax.axis_size("energy")
    energy = ENERGY_LOW + ENERGY_SPAN * (energy_slot.astype(jnp.float32) + 0.5) / grid_total
    prev_hop = passed_along(ham_hop[-1], "transpor", 1)
    levels = jnp.full((1, orbitals), energy[0])
    shift, loss = onsite_shift[0], onsite_loss[0]

    carry = jnp.zeros((4, orbitals, orbitals), jnp.float32)
    kept = (carry, carry, carry)
    for stage in range(half):
        active = (my_index == stage) | (my_index == partitions - 1 - stage)
        body = functools.partial(eliminate_kernel, stage == 0, partitions)
        eliminate = call(body, (4, 4, 4), orbitals)
        kept = lax.cond(
            active,
            lambda now, then, eliminate=eliminate: tuple(
                eliminate(now, ham_diag, ham_hop, prev_hop, inject, shift, loss, levels)
            ),
            lambda now, then: then,
            carry,
            kept,
        )
        other = partitions - 1 - stage
        if stage < half - 1:
            pairs = [(stage, stage + 1), (other, other - 1)]
        else:
            pairs = [(stage, other), (other, stage)]
        carry = lax.ppermute(kept[1], "transpor", pairs)
    first, second, reduced = kept
    join = call(functools.partial(join_kernel, partitions), (2, 2), orbitals)
    value_b, value_a = join(carry, reduced, first, ham_hop, prev_hop)
    for stage in range(half - 2, -1, -1):
        other = partitions - 1 - stage
        passed = lax.ppermute(value_a, "transpor", [(stage + 1, stage), (other - 1, other)])
        new_b, new_a = call(back_kernel, (2, 2), orbitals, False)(passed, second, first)
        active = (my_index == stage) | (my_index == other)
        value_b = jnp.where(active, new_b, value_b)
        value_a = jnp.where(active, new_a, value_a)
    occupied = 1.0 / (1.0 + jnp.exp((energy[0] - chemical[None, :]) / THERMAL))
    weight = jnp.concatenate([occupied, 1.0 - occupied], axis=0)
    slot = jnp.full((1, LANES), energy_slot[0].astype(jnp.float32))
    return exchange(value_a, value_b, weight, slot, grid_total, half)


def solution(mesh):
    in_specs = (
        P("transpor", None, None, None),
        P("transpor", None, None, None),
        P("transpor", None, None, None),
        P(),
        P("energy"),
        P("energy", "transpor", None),
        P("energy", "transpor", None),
    )
    out_specs = P("energy", "transpor", None, None, None)
    return jax.shard_map(
        per_device, mesh=mesh, in_specs=in_specs, out_specs=out_specs, check_vma=False
    )
```

profile of v0, /device:TPU:0, one launch (start us, length us, event | category | flops | bytes accessed | tf_op | source)
XLA Modules:
  0.0 111.2 jit_solution(7836264037981703509)
XLA Ops:
  0.0 0.0 copy-start
  0.0 1.1 slice_bitcast_fusion
  1.1 2.4 %collective-permute-start = (f32[2,192,192]{2,1,0:T(8,128)S(1)}, f32[2,192,192]{2,1,0:T(8,128)S(1)}, u32[]{:S(2)}, u32[]{:S(2)}) collective-permute-start(f32[2,192,192]{2,1,0:T(8,128)S(1)} %slice_bitcast_fusion), channel_id=1, source_target_pairs={{0,1},{1,2},{2,3},{4,5},{5,6},{6,7},{8,9},{9,10},{10,11},{12,13},{... | collective-permute-start | bytes 884744 | tf_op jit(solution)/shard_map/ppermute | solution.py:430
  4.1 0.0 copy-start.3
  4.2 0.6 collective-permute-done.prev
  4.8 0.0 copy-start.2
  4.8 0.0 copy-done
  4.8 0.0 copy-done.3
  4.8 0.6 copy-done.2
  5.5 23.5 %conditional.2 = ((f32[4,192,192]{2,1,0:T(8,128)S(1)}, f32[4,192,192]{2,1,0:T(8,128)S(1)}, f32[4,192,192]{2,1,0:T(8,128)S(1)})) conditional(s32[]{:T(128)} %convert_element_type.14, () %tuple.17, (f32[2,2,192,192]{3,2,1,0:T(8,128)}, f32[2,2,192,192]{3,2,1,0:T(8,128)S(1)}, f32[2,192,192]{2,1,0:T(8,128)S(1)}, f32[2,2,192,192]{3,2,1,0:T(8,128)}, ...), branch_computations={%region_0.0_spmd, %region_1.0_spmd} | conditional | bytes 2949160 | solution.py:451
  5.5 0.0 copy-start.1
  5.5 0.1 broadcast_in_dim.11.carry
  5.5 1.1 copy-done.1
  6.6 22.3 %branch_1_fun.2 = (f32[4,192,192]{2,1,0:T(8,128)S(1)}, f32[4,192,192]{2,1,0:T(8,128)S(1)}, f32[4,192,192]{2,1,0:T(8,128)S(1)}) custom-call(f32[4,192,192]{2,1,0:T(8,128)S(1)} %broadcast_in_dim.11.carry, f32[2,2,192,192]{3,2,1,0:T(8,128)S(1)} %copy-done.1, f32[2,2,192,192]{3,2,1,0:T(8,128)S(1)} %get-tuple-element.42.hop, ...), custom_call_target="tpu_custom_call" | custom-call | tf_op jit(solution)/shard_map/cond/branch_1_fun/pallas_call | solution.py:454
  28.9 2.2 %collective-permute-start.1 = (f32[4,192,192]{2,1,0:T(8,128)S(1)}, f32[4,192,192]{2,1,0:T(8,128)}, u32[]{:S(2)}, u32[]{:S(2)}) collective-permute-start(f32[4,192,192]{2,1,0:T(8,128)S(1)} %get-tuple-element.64), channel_id=1, source_target_pairs={{0,1},{3,2},{4,5},{7,6},{8,9},{11,10},{12,13},{15,14},{16,17},{19,... | collective-permute-start | bytes 1769480 | tf_op jit(solution)/shard_map/ppermute | solution.py:465
  31.1 1.1 %collective-permute-done.1 = f32[4,192,192]{2,1,0:T(8,128)} collective-permute-done((f32[4,192,192]{2,1,0:T(8,128)S(1)}, f32[4,192,192]{2,1,0:T(8,128)}, u32[]{:S(2)}, u32[]{:S(2)}) %collective-permute-start.1) | collective-permute-done | bytes 589856 | tf_op jit(solution)/shard_map/ppermute | solution.py:465
  32.3 0.7 collective-permute-start.2
  33.0 0.0 collective-permute-done.2.carry
  33.0 11.6 %shard_map.73 = (f32[2,192,192]{2,1,0:T(8,128)S(1)}, f32[2,192,192]{2,1,0:T(8,128)S(1)}) custom-call(f32[4,192,192]{2,1,0:T(8,128)S(1)} %collective-permute-done.2.carry, f32[4,192,192]{2,1,0:T(8,128)S(1)} %get-tuple-element.66.reduced, f32[4,192,192]{2,1,0:T(8,128)S(1)} %get-tuple-element.67.first, f32[2,2,192,192]{3,2,1,0:T(8,128)S(1)} %copy-done, ...), custom_call_target="tpu_custom_call" | custom-call | tf_op jit(solution)/shard_map/pallas_call | solution.py:468
  44.6 0.0 copy-start.4
  44.6 1.3 %collective-permute-start.3 = (f32[2,192,192]{2,1,0:T(8,128)S(1)}, f32[2,192,192]{2,1,0:T(8,128)S(1)}, u32[]{:S(2)}, u32[]{:S(2)}) collective-permute-start(f32[2,192,192]{2,1,0:T(8,128)S(1)} %get-tuple-element.68), channel_id=1, source_target_pairs={{1,0},{2,3},{5,4},{6,7},{9,8},{10,11},{13,12},{14,15},{17,16},{18,... | collective-permute-start | bytes 884744 | tf_op jit(solution)/shard_map/ppermute | solution.py:471
  45.9 0.0 copy-done.4
  45.9 36.7 %collective-permute-done.3.value = f32[2,192,192]{2,1,0:T(8,128)S(1)} collective-permute-done((f32[2,192,192]{2,1,0:T(8,128)S(1)}, f32[2,192,192]{2,1,0:T(8,128)S(1)}, u32[]{:S(2)}, u32[]{:S(2)}) %collective-permute-start.3) | collective-permute-done | bytes 294944 | tf_op jit(solution)/shard_map/ppermute | solution.py:471
  82.6 0.8 shard_map.74
  83.4 0.1 broadcast_select_fusion
  83.5 26.7 %shard_map.75 = f32[1,2,2,192,192]{4,3,2,1,0:T(8,128)S(1)} custom-call(f32[2,192,192]{2,1,0:T(8,128)S(1)} %get-tuple-element.75.value_a, f32[2,192,192]{2,1,0:T(8,128)S(1)} %get-tuple-element.74.value_b, f32[2,192]{1,0:T(2,128)S(1)} %pad_maximum_fusion.weight, f32[1,128]{1,0:T(1,128)S(1)} %broadcast_in_dim.17.slot), custom_call_target="tpu_custom_call" | custom-call | tf_op jit(solution)/shard_map/pallas_call | solution.py:396
  110.3 0.9 copy.22
  (5 shorter events, 0.0 us)
Async XLA Ops:
  0.0 4.8 %copy-start = (f32[2,2,192,192]{3,2,1,0:T(8,128)S(1)}, f32[2,2,192,192]{3,2,1,0:T(8,128)}, u32[]{:S(2)}) copy-start(f32[2,2,192,192]{3,2,1,0:T(8,128)} %hop.1) | copy-start | bytes 1769476
  1.1 3.7 %collective-permute-start = (f32[2,192,192]{2,1,0:T(8,128)S(1)}, f32[2,192,192]{2,1,0:T(8,128)S(1)}, u32[]{:S(2)}, u32[]{:S(2)}) collective-permute-start(f32[2,192,192]{2,1,0:T(8,128)S(1)} %slice_bitcast_fusion), channel_id=1, source_target_pairs={{0,1},{1,2},{2,3},{4,5},{5,6},{6,7},{8,9},{9,10},{10,11},{12,13},{... | collective-permute-start | bytes 884744 | tf_op jit(solution)/shard_map/ppermute | solution.py:430
  4.1 0.7 copy-start.3
  4.8 0.7 copy-start.2
  5.5 1.1 %copy-start.1 = (f32[2,2,192,192]{3,2,1,0:T(8,128)S(1)}, f32[2,2,192,192]{3,2,1,0:T(8,128)}, u32[]{:S(2)}) copy-start(f32[2,2,192,192]{3,2,1,0:T(8,128)} %get-tuple-element.41.diag) | copy-start | bytes 1769476 | tf_op jit(solution)/shard_map/cond
  28.9 3.3 %collective-permute-start.1 = (f32[4,192,192]{2,1,0:T(8,128)S(1)}, f32[4,192,192]{2,1,0:T(8,128)}, u32[]{:S(2)}, u32[]{:S(2)}) collective-permute-start(f32[4,192,192]{2,1,0:T(8,128)S(1)} %get-tuple-element.64), channel_id=1, source_target_pairs={{0,1},{3,2},{4,5},{7,6},{8,9},{11,10},{12,13},{15,14},{16,17},{19,... | collective-permute-start | bytes 1769480 | tf_op jit(solution)/shard_map/ppermute | solution.py:465
  32.3 0.7 collective-permute-start.2
  44.6 1.3 %copy-start.4 = (f32[192]{0:T(256)S(1)}, f32[192]{0:T(256)}, u32[]{:S(2)}) copy-start(f32[192]{0:T(256)} %param.14) | copy-start | bytes 2308
  44.6 38.0 %collective-permute-start.3 = (f32[2,192,192]{2,1,0:T(8,128)S(1)}, f32[2,192,192]{2,1,0:T(8,128)S(1)}, u32[]{:S(2)}, u32[]{:S(2)}) collective-permute-start(f32[2,192,192]{2,1,0:T(8,128)S(1)} %get-tuple-element.68), channel_id=1, source_target_pairs={{1,0},{2,3},{5,4},{6,7},{9,8},{10,11},{13,12},{14,15},{17,16},{18,... | collective-permute-start | bytes 884744 | tf_op jit(solution)/shard_map/ppermute | solution.py:471
where the time goes:
time: 113 us; the launch traced here: 111 us
  Pallas kernels  61.4 us (54%)
  waiting for transfers between devices  38.4 us (34%)
  starting transfers between devices  6.57 us (6%)
  local copies, waits for them, and re-layouts  3.8 us (3%)
    ppermute x1, waiting for transfers between devices, per_device(): lax.ppermute(value_a, 'transpor', [(stage + 1, stage), (other - 1, other)])  36.7 us
    pallas_call x1, Pallas kernels, exchange(): pl.pallas_call(functools.partial(exchange_kernel, count, half_way), out_s...  26.7 us
    pallas_call x1, Pallas kernels, per_device(): eliminate(now, ham_diag, ham_hop, prev_hop, inject, shift, loss, levels)  22.3 us
    pallas_call x1, Pallas kernels, per_device(): value_b, value_a = join(carry, reduced, first, ham_hop, prev_hop)  11.6 us
    ppermute x2, starting transfers between devices, per_device(): carry = lax.ppermute(kept[1], 'transpor', pairs)  2.9 us
    ppermute x1, starting transfers between devices, passed_along(): return lax.ppermute(x, axis, pairs)  2.38 us
  transfers between devices with their start and end apart: 4, of which 3 were waited for; matrix products, arithmetic and copies ran while one was open for 0% of the time, Pallas kernels for 0%

commit v1 on v0

--- a/solution.py
+++ b/solution.py
@@ -151,8 +151,8 @@
     )
 
 
-def eliminate_kernel(starts, partitions, carry, diag, hop, prev, inject, shift, loss, energy,
-                     first_out, second_out, reduced_out, x_ref):
+def eliminate_kernel(starts, partitions, carry_on, carry_held, diag, hop, prev, inject, shift,
+                     loss, energy, first_out, on_out, held_out, reduced_out, x_ref):
     my_index = lax.axis_index("transpor")
     left = my_index < partitions // 2
     is_last = jnp.where(my_index == partitions - 1, 1.0, 0.0)
@@ -175,8 +175,8 @@
     source = pick(left, sources[0], sources[1])
     if not starts:
         back = ready(low_a())
-        pivot = minus(pivot, cmul_ready(back, ready(take(carry, 0))))
-        source = minus(source, cmul_ready(back, ready(take(carry, 2))))
+        pivot = minus(pivot, cmul_ready(back, ready(take(carry_on, 0))))
+        source = minus(source, cmul_ready(back, ready(take(carry_held, 0))))
     put(reduced_out, 0, pick(left, blocks[1], blocks[0]))
     inverse = ready(invert(pivot, x_ref))
     on = cmul_ready(inverse, ready(up_a()))
@@ -189,25 +189,31 @@
     put(reduced_out, 0, pivot)
     put(reduced_out, 2, source)
     inverse = ready(invert(pivot, x_ref))
-    put(second_out, 0, cmul_ready(inverse, ready(up_b())))
-    put(second_out, 2, cmul_ready(inverse, ready(source)))
-
-
-def join_kernel(partitions, carry, reduced, first, hop, prev, value_out, first_value_out, x_ref):
+    put(on_out, 0, cmul_ready(inverse, ready(up_b())))
+    put(held_out, 0, cmul_ready(inverse, ready(source)))
+
+
+def join_inverse_kernel(partitions, carry_on, reduced, hop, prev, inverse_out, x_ref):
     left = lax.axis_index("transpor") < partitions // 2
     on = ready(couplings(left, hop, prev)[3]())
-    pivot = minus(take(reduced, 0), cmul_ready(on, ready(take(carry, 0))))
-    source = minus(take(reduced, 2), cmul_ready(on, ready(take(carry, 2))))
-    inverse = ready(invert(pivot, x_ref))
-    value = cmul_ready(inverse, ready(source))
+    pivot = minus(take(reduced, 0), cmul_ready(on, ready(take(carry_on, 0))))
+    put(inverse_out, 0, invert(pivot, x_ref))
+
+
+def join_value_kernel(partitions, carry_held, inverse, reduced, first, hop, prev,
+                      value_out, first_value_out):
+    left = lax.axis_index("transpor") < partitions // 2
+    on = ready(couplings(left, hop, prev)[3]())
+    source = minus(take(reduced, 2), cmul_ready(on, ready(take(carry_held, 0))))
+    value = cmul_ready(ready(take(inverse, 0)), ready(source))
     put(value_out, 0, value)
     change = cmul_ready(ready(take(first, 0)), ready(value))
     put(first_value_out, 0, minus(take(first, 2), change))
 
 
-def back_kernel(value, second, first, second_out, first_out):
-    change = cmul_ready(ready(take(second, 0)), ready(take(value, 0)))
-    result = minus(take(second, 2), change)
+def back_kernel(value, on, held, first, second_out, first_out):
+    change = cmul_ready(ready(take(on, 0)), ready(take(value, 0)))
+    result = minus(take(held, 0), change)
     put(second_out, 0, result)
     change = cmul_ready(ready(take(first, 0)), ready(result))
     put(first_out, 0, minus(take(first, 2), change))
@@ -414,13 +420,18 @@
     )(value_a, value_b, weight, slot)
 
 
-def call(body, counts, order, scratch=True):
+def call(body, counts, order, scratch=True, inverses=0):
     shapes = [jax.ShapeDtypeStruct((count, order, order), jnp.float32) for count in counts]
     return pl.pallas_call(
         body,
         out_shape=shapes,
         scratch_shapes=[pltpu.VMEM((2, order, order), jnp.float32)] if scratch else [],
         compiler_params=pltpu.CompilerParams(vmem_limit_bytes=48 * 1024 * 1024),
+        cost_estimate=pl.CostEstimate(
+            flops=(4 + 22 * inverses) * 18 * order**3,
+            bytes_accessed=64 * order**2,
+            transcendentals=0,
+        ),
     )
 
 
@@ -442,19 +453,22 @@
     levels = jnp.full((1, orbitals), energy[0])
     shift, loss = onsite_shift[0], onsite_loss[0]
 
-    carry = jnp.zeros((4, orbitals, orbitals), jnp.float32)
-    kept = (carry, carry, carry)
+    four = jnp.zeros((4, orbitals, orbitals), jnp.float32)
+    two = jnp.zeros((2, orbitals, orbitals), jnp.float32)
+    carry_on = carry_held = two
+    kept = (four, two, two, four)
     for stage in range(half):
         active = (my_index == stage) | (my_index == partitions - 1 - stage)
         body = functools.partial(eliminate_kernel, stage == 0, partitions)
-        eliminate = call(body, (4, 4, 4), orbitals)
+        eliminate = call(body, (4, 2, 2, 4), orbitals, inverses=2)
         kept = lax.cond(
             active,
-            lambda now, then, eliminate=eliminate: tuple(
-                eliminate(now, ham_diag, ham_hop, prev_hop, inject, shift, loss, levels)
+            lambda on, held, then, eliminate=eliminate: tuple(
+                eliminate(on, held, ham_diag, ham_hop, prev_hop, inject, shift, loss, levels)
             ),
-            lambda now, then: then,
-            carry,
+            lambda on, held, then: then,
+            carry_on,
+            carry_held,
             kept,
         )
         other = partitions - 1 - stage
@@ -462,14 +476,22 @@
             pairs = [(stage, stage + 1), (other, other - 1)]
         else:
             pairs = [(stage, other), (other, stage)]
-        carry = lax.ppermute(kept[1], "transpor", pairs)
-    first, second, reduced = kept
-    join = call(functools.partial(join_kernel, partitions), (2, 2), orbitals)
-    value_b, value_a = join(carry, reduced, first, ham_hop, prev_hop)
+        carry_on = lax.ppermute(kept[1], "transpor", pairs)
+        sent = kept[2]
+        if stage == half - 1:
+            carry_on, sent = lax.optimization_barrier((carry_on, sent))
+        carry_held = lax.ppermute(sent, "transpor", pairs)
+    first, on, held, reduced = kept
+    join_inverse = call(
+        functools.partial(join_inverse_kernel, partitions), (2,), orbitals, inverses=1
+    )
+    join_value = call(functools.partial(join_value_kernel, partitions), (2, 2), orbitals, False)
+    (inverse,) = join_inverse(carry_on, reduced, ham_hop, prev_hop)
+    value_b, value_a = join_value(carry_held, inverse, reduced, first, ham_hop, prev_hop)
     for stage in range(half - 2, -1, -1):
         other = partitions - 1 - stage
         passed = lax.ppermute(value_a, "transpor", [(stage + 1, stage), (other - 1, other)])
-        new_b, new_a = call(back_kernel, (2, 2), orbitals, False)(passed, second, first)
+        new_b, new_a = call(back_kernel, (2, 2), orbitals, False)(passed, on, held, first)
         active = (my_index == stage) | (my_index == other)
         value_b = jnp.where(active, new_b, value_b)
         value_a = jnp.where(active, new_a, value_a)

time: 113 us -> 114 us (level); the launches traced: 111 us -> 113 us
  Pallas kernels: 61.4 us -> 64.7 us
  starting transfers between devices: 6.57 us -> 9.11 us
  waiting for transfers between devices: 38.4 us -> 36 us
    pallas_call x1, Pallas kernels: 26.7 us -> 29.3 us  [exchange(): pl.pallas_call(functools.partial(exchange_kernel, count, half_way), out_s...]
    ppermute x2 -> x4, starting transfers between devices: 2.9 us -> 5.44 us  [the longest x2 2.72 us: per_device(): carry_on = lax.ppermute(kept[1], 'transpor', pairs)]
    ppermute x1, waiting for transfers between devices: 36.7 us -> 34.7 us  [per_device(): lax.ppermute(value_a, 'transpor', [(stage + 1, stage), (other - 1, other)])]
    pallas_call x3 -> x4, Pallas kernels: 34.7 us -> 35.4 us  [the longest x1 22.6 us: per_device(): eliminate(on, held, ham_diag, ham_hop, prev_hop, inject, shift, loss, lev...]
  transfers between devices with their start and end apart: 4 -> 6, of which waited for: 3 -> 3; matrix products, arithmetic and copies ran while one was open for 0% -> 0% of each run, Pallas kernels for 0% -> 10%
where the time goes in v1:
time: 114 us; the launch traced here: 113 us
  Pallas kernels  64.7 us (57%)
  waiting for transfers between devices  36 us (32%)
  starting transfers between devices  9.11 us (8%)
  local copies, waits for them, and re-layouts  2.7 us (2%)
    ppermute x1, waiting for transfers between devices, per_device(): lax.ppermute(value_a, 'transpor', [(stage + 1, stage), (other - 1, other)])  34.7 us
    pallas_call x1, Pallas kernels, exchange(): pl.pallas_call(functools.partial(exchange_kernel, count, half_way), out_s...  29.3 us
    pallas_call x1, Pallas kernels, per_device(): eliminate(on, held, ham_diag, ham_hop, prev_hop, inject, shift, loss, lev...  22.6 us
    pallas_call x1, Pallas kernels, per_device(): inverse, = join_inverse(carry_on, reduced, ham_hop, prev_hop)  10.8 us
    ppermute x2, starting transfers between devices, per_device(): carry_on = lax.ppermute(kept[1], 'transpor', pairs)  2.72 us
    ppermute x2, starting transfers between devices, per_device(): carry_held = lax.ppermute(sent, 'transpor', pairs)  2.72 us
    ppermute x1, starting transfers between devices, passed_along(): return lax.ppermute(x, axis, pairs)  2.38 us
  transfers between devices with their start and end apart: 6, of which 3 were waited for; matrix products, arithmetic and copies ran while one was open for 0% of the time, Pallas kernels for 10%

profile of v1, /device:TPU:0, one launch (start us, length us, event | category | flops | bytes accessed | tf_op | source)
XLA Modules:
  0.0 113.5 jit_solution(10838575648354889530)
XLA Ops:
  0.0 0.0 copy-start
  0.0 1.1 slice_bitcast_fusion
  1.1 2.4 %collective-permute-start = (f32[2,192,192]{2,1,0:T(8,128)S(1)}, f32[2,192,192]{2,1,0:T(8,128)S(1)}, u32[]{:S(2)}, u32[]{:S(2)}) collective-permute-start(f32[2,192,192]{2,1,0:T(8,128)S(1)} %slice_bitcast_fusion), channel_id=1, source_target_pairs={{0,1},{1,2},{2,3},{4,5},{5,6},{6,7},{8,9},{9,10},{10,11},{12,13},{... | collective-permute-start | bytes 884744 | tf_op jit(solution)/shard_map/ppermute | solution.py:441
  4.1 0.0 copy-start.3
  4.2 0.6 collective-permute-done.prev
  4.8 0.0 copy-start.2
  4.8 0.0 copy-done
  4.8 0.0 copy-done.3
  4.8 0.6 copy-done.2
  5.5 22.6 %conditional.2 = ((f32[4,192,192]{2,1,0:T(8,128)S(1)}, f32[2,192,192]{2,1,0:T(8,128)S(1)}, f32[2,192,192]{2,1,0:T(8,128)S(1)}, f32[4,192,192]{2,1,0:T(8,128)S(1)})) conditional(s32[]{:T(128)} %convert_element_type.14, () %tuple.18, (f32[2,2,192,192]{3,2,1,0:T(8,128)}, f32[2,2,192,192]{3,2,1,0:T(8,128)S(1)}, f32[2,192,192]{2,1,0:T(8,128)S(1)}, ...), branch_computations={%region_0.0_spmd, %region_1.0_spmd} | conditional | flops 6115295232 | bytes 2654220 | solution.py:464
  5.5 22.6 %branch_1_fun.2 = (f32[4,192,192]{2,1,0:T(8,128)S(1)}, f32[2,192,192]{2,1,0:T(8,128)S(1)}, f32[2,192,192]{2,1,0:T(8,128)S(1)}, f32[4,192,192]{2,1,0:T(8,128)S(1)}) custom-call(f32[2,192,192]{2,1,0:T(8,128)S(1)} %broadcast_in_dim.14.carry_on.carry_held, f32[2,192,192]{2,1,0:T(8,128)S(1)} %broadcast_in_dim.14.carry_on.carry_held, ...), custom_call_target="tpu_custom_call" | custom-call | flops 6115295232 | bytes 2359296 | tf_op jit(solution)/shard_map/cond/branch_1_fun/pallas_call | solution.py:467
  28.1 2.1 %collective-permute-start.1 = (f32[2,192,192]{2,1,0:T(8,128)S(1)}, f32[2,192,192]{2,1,0:T(8,128)}, u32[]{:S(2)}, u32[]{:S(2)}) collective-permute-start(f32[2,192,192]{2,1,0:T(8,128)S(1)} %get-tuple-element.73), channel_id=1, source_target_pairs={{0,1},{3,2},{4,5},{7,6},{8,9},{11,10},{12,13},{15,14},{16,17},{19,... | collective-permute-start | bytes 884744 | tf_op jit(solution)/shard_map/ppermute | solution.py:479
  30.2 2.0 %collective-permute-start.2 = (f32[2,192,192]{2,1,0:T(8,128)S(1)}, f32[2,192,192]{2,1,0:T(8,128)}, u32[]{:S(2)}, u32[]{:S(2)}) collective-permute-start(f32[2,192,192]{2,1,0:T(8,128)S(1)} %get-tuple-element.74), channel_id=1, source_target_pairs={{0,1},{3,2},{4,5},{7,6},{8,9},{11,10},{12,13},{15,14},{16,17},{19,... | collective-permute-start | bytes 884744 | tf_op jit(solution)/shard_map/ppermute | solution.py:483
  32.2 0.0 collective-permute-done.1
  32.2 0.7 collective-permute-done.2
  32.9 0.7 collective-permute-start.3
  33.6 0.0 collective-permute-done.3.carry_on
  33.6 0.7 collective-permute-start.4
  34.3 10.8 %shard_map.73.inverse = f32[2,192,192]{2,1,0:T(8,128)S(1)} custom-call(f32[2,192,192]{2,1,0:T(8,128)S(1)} %collective-permute-done.3.carry_on, f32[4,192,192]{2,1,0:T(8,128)S(1)} %get-tuple-element.79.reduced, f32[2,2,192,192]{3,2,1,0:T(8,128)S(1)} %copy-done, f32[2,192,192]{2,1,0:T(8,128)S(1)} %collective-permute-done.prev), custom_call_target="tpu_custom_call" | custom-call | flops 3312451584 | bytes 2359296 | tf_op jit(solution)/shard_map/pallas_call | solution.py:489
  45.1 0.0 collective-permute-done.4.carry_held
  45.1 1.2 %shard_map.74 = (f32[2,192,192]{2,1,0:T(8,128)S(1)}, f32[2,192,192]{2,1,0:T(8,128)S(1)}) custom-call(f32[2,192,192]{2,1,0:T(8,128)S(1)} %collective-permute-done.4.carry_held, f32[2,192,192]{2,1,0:T(8,128)S(1)} %shard_map.73.inverse, f32[4,192,192]{2,1,0:T(8,128)S(1)} %get-tuple-element.79.reduced, f32[4,192,192]{2,1,0:T(8,128)S(1)} %get-tuple-element.80.first, ...), custom_call_target="tpu_custom_call" | custom-call | flops 509607936 | bytes 2359296 | tf_op jit(solution)/shard_map/pallas_call | solution.py:490
  46.3 0.0 copy-start.1
  46.4 1.3 %collective-permute-start.5 = (f32[2,192,192]{2,1,0:T(8,128)S(1)}, f32[2,192,192]{2,1,0:T(8,128)S(1)}, u32[]{:S(2)}, u32[]{:S(2)}) collective-permute-start(f32[2,192,192]{2,1,0:T(8,128)S(1)} %get-tuple-element.81), channel_id=1, source_target_pairs={{1,0},{2,3},{5,4},{6,7},{9,8},{10,11},{13,12},{14,15},{17,16},{18,... | collective-permute-start | bytes 884744 | tf_op jit(solution)/shard_map/ppermute | solution.py:493
  47.7 0.0 copy-done.1
  47.7 34.7 %collective-permute-done.5.value = f32[2,192,192]{2,1,0:T(8,128)S(1)} collective-permute-done((f32[2,192,192]{2,1,0:T(8,128)S(1)}, f32[2,192,192]{2,1,0:T(8,128)S(1)}, u32[]{:S(2)}, u32[]{:S(2)}) %collective-permute-start.5) | collective-permute-done | bytes 294944 | tf_op jit(solution)/shard_map/ppermute | solution.py:493
  82.4 0.8 shard_map.75
  83.2 0.1 broadcast_select_fusion
  83.3 29.3 %shard_map.76 = f32[1,2,2,192,192]{4,3,2,1,0:T(8,128)S(1)} custom-call(f32[2,192,192]{2,1,0:T(8,128)S(1)} %get-tuple-element.88.value_a, f32[2,192,192]{2,1,0:T(8,128)S(1)} %get-tuple-element.87.value_b, f32[2,192]{1,0:T(2,128)S(1)} %pad_maximum_fusion.weight, f32[1,128]{1,0:T(1,128)S(1)} %broadcast_in_dim.20.slot), custom_call_target="tpu_custom_call" | custom-call | tf_op jit(solution)/shard_map/pallas_call | solution.py:402
  112.6 0.9 copy.26
  (6 shorter events, 0.1 us)
Async XLA Ops:
  0.0 4.8 %copy-start = (f32[2,2,192,192]{3,2,1,0:T(8,128)S(1)}, f32[2,2,192,192]{3,2,1,0:T(8,128)}, u32[]{:S(2)}) copy-start(f32[2,2,192,192]{3,2,1,0:T(8,128)} %hop.3) | copy-start | bytes 1769476
  1.1 3.7 %collective-permute-start = (f32[2,192,192]{2,1,0:T(8,128)S(1)}, f32[2,192,192]{2,1,0:T(8,128)S(1)}, u32[]{:S(2)}, u32[]{:S(2)}) collective-permute-start(f32[2,192,192]{2,1,0:T(8,128)S(1)} %slice_bitcast_fusion), channel_id=1, source_target_pairs={{0,1},{1,2},{2,3},{4,5},{5,6},{6,7},{8,9},{9,10},{10,11},{12,13},{... | collective-permute-start | bytes 884744 | tf_op jit(solution)/shard_map/ppermute | solution.py:441
  4.1 0.7 copy-start.3
  4.8 0.7 copy-start.2
  28.1 4.1 %collective-permute-start.1 = (f32[2,192,192]{2,1,0:T(8,128)S(1)}, f32[2,192,192]{2,1,0:T(8,128)}, u32[]{:S(2)}, u32[]{:S(2)}) collective-permute-start(f32[2,192,192]{2,1,0:T(8,128)S(1)} %get-tuple-element.73), channel_id=1, source_target_pairs={{0,1},{3,2},{4,5},{7,6},{8,9},{11,10},{12,13},{15,14},{16,17},{19,... | collective-permute-start | bytes 884744 | tf_op jit(solution)/shard_map/ppermute | solution.py:479
  30.2 2.8 %collective-permute-start.2 = (f32[2,192,192]{2,1,0:T(8,128)S(1)}, f32[2,192,192]{2,1,0:T(8,128)}, u32[]{:S(2)}, u32[]{:S(2)}) collective-permute-start(f32[2,192,192]{2,1,0:T(8,128)S(1)} %get-tuple-element.74), channel_id=1, source_target_pairs={{0,1},{3,2},{4,5},{7,6},{8,9},{11,10},{12,13},{15,14},{16,17},{19,... | collective-permute-start | bytes 884744 | tf_op jit(solution)/shard_map/ppermute | solution.py:483
  32.9 0.7 collective-permute-start.3
  33.6 11.5 %collective-permute-start.4 = (f32[2,192,192]{2,1,0:T(8,128)S(1)}, f32[2,192,192]{2,1,0:T(8,128)S(1)}, u32[]{:S(2)}, u32[]{:S(2)}) collective-permute-start(f32[2,192,192]{2,1,0:T(8,128)S(1)} %get-tuple-element.77.held), channel_id=1, source_target_pairs={{1,2},{2,1},{5,6},{6,5},{9,10},{10,9},{13,14},{14,13},{17,18},{18,... | collective-permute-start | bytes 884744 | tf_op jit(solution)/shard_map/ppermute | solution.py:483
  46.3 1.3 %copy-start.1 = (f32[192]{0:T(256)S(1)}, f32[192]{0:T(256)}, u32[]{:S(2)}) copy-start(f32[192]{0:T(256)} %param.14) | copy-start | bytes 2308
  46.4 36.0 %collective-permute-start.5 = (f32[2,192,192]{2,1,0:T(8,128)S(1)}, f32[2,192,192]{2,1,0:T(8,128)S(1)}, u32[]{:S(2)}, u32[]{:S(2)}) collective-permute-start(f32[2,192,192]{2,1,0:T(8,128)S(1)} %get-tuple-element.81), channel_id=1, source_target_pairs={{1,0},{2,3},{5,4},{6,7},{9,8},{10,11},{13,12},{14,15},{17,16},{18,... | collective-permute-start | bytes 884744 | tf_op jit(solution)/shard_map/ppermute | solution.py:493
